TPU v7x, 256 devices: a whole 4x4x8 slice. The times are simulated.
256 devices in a mesh: dp: 16 (over y, x), tensor: 16 (over z, core).
Axes of the slice: x: 4, y: 4, z: 8, core: 2. Of those that a mesh axis runs over, the one named last changes fastest.
Arguments:
- tokens: bfloat16 [1024, 8192], P('tensor', 'dp'), may hold values from -6 to 6
- gate_weight: bfloat16 [8192, 14336], P('dp', 'tensor'), may hold values from -0.0625 to 0.0625
- up_weight: bfloat16 [8192, 14336], P('dp', 'tensor'), may hold values from -0.0625 to 0.0625
- down_weight: bfloat16 [14336, 8192], P('tensor', 'dp'), may hold values from -0.046875 to 0.046875
- out_grad: bfloat16 [1024, 8192], P('tensor', 'dp'), may hold values from -6 to 6
Outputs:
- ffn_output: bfloat16 [1024, 8192], P('tensor', 'dp')
- input_grad: bfloat16 [1024, 8192], P('tensor', 'dp')
- gate_weight_grad: float32 [8192, 14336], P('dp', 'tensor')
- up_weight_grad: float32 [8192, 14336], P('dp', 'tensor')
- down_weight_grad: float32 [14336, 8192], P('tensor', 'dp')
All inputs are finite; a program needn't handle non-finite values.
Results may differ from a plain program's by a relative error of at most 0.0049.
Values may be sent and summed in bfloat16 or wider, within the bound.
No kernel may reach another device: no remote copies, remote signals or barrier semaphores. Data moves between devices by JAX's collectives and lax.ppermute only.
A program may use at most 128 MiB of HBM per device.

v0:
```python
import math

import jax
import jax.numpy as jnp
from jax import lax
from jax.sharding import PartitionSpec as P


def body(tokens, gate_weight, up_weight, down_weight, out_grad):
    hidden_width = gate_weight.shape[1]
    tokens_all = lax.all_gather(tokens, "tensor", axis=0, tiled=True)
    total_rows = tokens_all.shape[0]
    weights_both = jnp.concatenate([gate_weight, up_weight], 1)
    block = tokens_all
    projected = lax.psum_scatter(
        jnp.dot(block, weights_both, preferred_element_type=jnp.float32),
        "dp",
        scatter_dimension=0,
        tiled=True,
    )
    gate = projected[:, :hidden_width]
    up = projected[:, hidden_width:]
    hidden = (jax.nn.sigmoid(gate) * gate * up).astype(jnp.bfloat16)
    hidden_all = lax.all_gather(hidden, "dp", axis=0, tiled=True)
    block = hidden_all
    ffn_output = lax.psum_scatter(
        jnp.dot(block, down_weight, preferred_element_type=jnp.float32),
        "tensor",
        scatter_dimension=0,
        tiled=True,
    ).astype(jnp.bfloat16)
    grad_all = lax.all_gather(out_grad, "tensor", axis=0, tiled=True)
    block = grad_all
    hidden_grad = lax.psum_scatter(
        lax.dot_general(
            block, down_weight, (((1,), (1,)), ((), ())), preferred_element_type=jnp.float32
        ),
        "dp",
        scatter_dimension=0,
        tiled=True,
    )
    sigmoid_gate = jax.nn.sigmoid(gate)
    activated = gate * sigmoid_gate
    up_grad = (hidden_grad * activated).astype(jnp.bfloat16)
    gate_grad = (hidden_grad * up * sigmoid_gate * (1.0 + gate * (1.0 - sigmoid_gate))).astype(
        jnp.bfloat16
    )
    gate_grad_all, up_grad_all = (
        lax.all_gather(gate_grad, "dp", axis=0, tiled=True),
        lax.all_gather(up_grad, "dp", axis=0, tiled=True),
    )
    grads_both = jnp.concatenate([gate_grad_all, up_grad_all], 1)
    block = grads_both
    input_grad = lax.psum_scatter(
        lax.dot_general(
            block, weights_both, (((1,), (1,)), ((), ())), preferred_element_type=jnp.float32
        ),
        "tensor",
        scatter_dimension=0,
        tiled=True,
    ).astype(jnp.bfloat16)
    factor = 1.0 / math.sqrt(total_rows)
    weight_grads = (
        lax.dot_general(
            tokens_all, grads_both, (((0,), (0,)), ((), ())), preferred_element_type=jnp.float32
        )
        * factor
    )
    gate_weight_grad = weight_grads[:, :hidden_width]
    up_weight_grad = weight_grads[:, hidden_width:]
    down_weight_grad = (
        lax.dot_general(
            hidden_all, grad_all, (((0,), (0,)), ((), ())), preferred_element_type=jnp.float32
        )
        * factor
    )
    return (ffn_output, input_grad, gate_weight_grad, up_weight_grad, down_weight_grad)


def solution(mesh):
    return jax.shard_map(
        body,
        mesh=mesh,
        in_specs=(
            P("tensor", "dp"),
            P("dp", "tensor"),
            P("dp", "tensor"),
            P("tensor", "dp"),
            P("tensor", "dp"),
        ),
        out_specs=(
            P("tensor", "dp"),
            P("tensor", "dp"),
            P("dp", "tensor"),
            P("dp", "tensor"),
            P("tensor", "dp"),
        ),
        check_vma=False,
    )
```

profile of v0, /device:TPU:1, one launch (start us, length us, event | category | flops | bytes accessed | tf_op | source)
XLA Modules:
  0.0 548.9 jit_solution(4212866981050804907)
XLA Ops:
  7.2 0.0 copy-start
  7.2 0.0 all-gather.10.cloned.1.call-start
  7.2 0.7 all-gather.10.cloned.1.call-update
  7.9 0.0 all-gather.6.cloned.1.call-start
  8.0 0.7 all-gather.6.cloned.1.call-update
  8.7 0.0 reduce-scatter.15.cloned.1.call-start
  8.7 44.0 %all-gather.10.cloned.1.call-done = bf16[1024,512]{1,0:T(8,128)(2,1)} async-done(((bf16[64,512]{1,0:T(8,128)(2,1)}), bf16[1024,512]{1,0:T(8,128)(2,1)}) %all-gather.10.cloned.1.call-update) | async-done | bytes 1048592 | tf_op jit(solution)/shard_map/all_gather | solution.py:32
  52.7 0.0 copy-done
  52.7 4.3 fusion.3
  57.0 0.0 reduce-scatter.15.cloned.1.call-update
  57.0 0.0 reduce-scatter.13.cloned.1.call-start
  57.1 1.1 copy-done.1
  58.2 1.0 constant_dynamic-update-slice_fusion.1
  59.2 1.0 constant_dynamic-update-slice_fusion
  60.2 31.6 %all-gather.6.cloned.1.call-done = bf16[1024,512]{1,0:T(8,128)(2,1)} async-done(((bf16[64,512]{1,0:T(8,128)(2,1)}), bf16[1024,512]{1,0:T(8,128)(2,1)}) %all-gather.6.cloned.1.call-update) | async-done | bytes 1048592 | tf_op jit(solution)/shard_map/all_gather | solution.py:11
  91.8 6.9 %convolution_bitcast_fusion = f32[1024,1792]{0,1:T(8,128)} fusion(bf16[512,1792]{1,0:T(8,128)(2,1)} %constant_dynamic-update-slice_fusion, bf16[1024,512]{1,0:T(8,128)(2,1)} %all-gather.6.cloned.1.call-done), kind=kOutput, calls=%fused_computation | convolution fusion | flops 1879048192 | bytes 10223616 | tf_op jit(solution)/shard_map/dot_general | solution.py:16
  98.7 8.4 %copy.27 = f32[1024,1792]{1,0:T(8,128)} copy(f32[1024,1792]{0,1:T(8,128)} %convolution_bitcast_fusion) | data formatting | bytes 14680064
  107.2 0.0 reduce-scatter.13.cloned.1.call-update
  107.2 0.0 all-gather.12.cloned.1.call-start
  107.2 66.4 %reduce-scatter.15.cloned.1.call-done = f32[64,896]{1,0:T(8,128)} async-done(((f32[1024,896]{1,0:T(8,128)}), f32[64,896]{1,0:T(8,128)}) %reduce-scatter.15.cloned.1.call-update) | async-done | bytes 229392 | tf_op jit(solution)/shard_map/reduce_scatter | solution.py:34
  173.7 91.5 %reduce-scatter.13.cloned.1.call-done = f32[64,1792]{1,0:T(8,128)} async-done(((f32[1024,1792]{1,0:T(8,128)}), f32[64,1792]{1,0:T(8,128)}) %reduce-scatter.13.cloned.1.call-update) | async-done | bytes 458768 | tf_op jit(solution)/shard_map/reduce_scatter | solution.py:15
  265.2 2.0 multiply_convert_fusion
  267.1 0.0 all-gather.12.cloned.1.call-update
  267.2 0.0 all-gather.14.cloned.1.call-start
  267.2 0.5 all-gather.14.cloned.1.call-update
  267.7 0.0 all-gather.8.cloned.1.call-start
  267.8 0.7 all-gather.8.cloned.1.call-update
  268.5 0.0 reduce-scatter.11.cloned.1.call-start
  268.5 48.6 %all-gather.12.cloned.1.call-done = bf16[1024,896]{1,0:T(8,128)(2,1)} async-done(((bf16[64,896]{1,0:T(8,128)(2,1)}), bf16[1024,896]{1,0:T(8,128)(2,1)}) %all-gather.12.cloned.1.call-update) | async-done | bytes 1835024 | tf_op jit(solution)/shard_map/all_gather | solution.py:49
  317.2 2.9 constant_dynamic-update-slice_fusion.3
  320.1 49.0 %all-gather.14.cloned.1.call-done = bf16[1024,896]{1,0:T(8,128)(2,1)} async-done(((bf16[64,896]{1,0:T(8,128)(2,1)}), bf16[1024,896]{1,0:T(8,128)(2,1)}) %all-gather.14.cloned.1.call-update) | async-done | bytes 1835024 | tf_op jit(solution)/shard_map/all_gather | solution.py:50
  369.1 2.9 constant_dynamic-update-slice_fusion.2
  372.0 6.0 %fusion.4 = f32[1024,512]{1,0:T(8,128)} fusion(bf16[1024,1792]{1,0:T(8,128)(2,1)} %constant_dynamic-update-slice_fusion.2, bf16[512,1792]{1,0:T(8,128)(2,1)} %constant_dynamic-update-slice_fusion), kind=kOutput, calls=%fused_computation.15 | convolution fusion | flops 1879048192 | bytes 7602176 | tf_op jit(solution)/shard_map/dot_general | solution.py:55
  378.1 0.0 reduce-scatter.11.cloned.1.call-update
  378.1 0.0 reduce-scatter.9.cloned.1.call-start
  378.2 42.5 %all-gather.8.cloned.1.call-done = bf16[1024,896]{1,0:T(8,128)(2,1)} async-done(((bf16[64,896]{1,0:T(8,128)(2,1)}), bf16[1024,896]{1,0:T(8,128)(2,1)}) %all-gather.8.cloned.1.call-update) | async-done | bytes 1835024 | tf_op jit(solution)/shard_map/all_gather | solution.py:24
  420.7 4.1 fusion.2
  424.7 0.0 reduce-scatter.9.cloned.1.call-update
  424.8 1.2 copy-done.3
  426.0 4.2 multiply_bitcast_fusion
  430.1 1.6 fusion.1
  431.7 2.7 copy.24
  434.5 1.7 copy.25
  436.1 4.1 convolution_multiply_fusion
  440.3 40.0 %reduce-scatter.11.cloned.1.call-done = f32[64,512]{1,0:T(8,128)} async-done(((f32[1024,512]{1,0:T(8,128)}), f32[64,512]{1,0:T(8,128)}) %reduce-scatter.11.cloned.1.call-update) | async-done | bytes 131088 | tf_op jit(solution)/shard_map/reduce_scatter | solution.py:54
  480.3 1.5 convert_element_type.19
  481.8 59.0 %reduce-scatter.9.cloned.1.call-done = f32[64,512]{1,0:T(8,128)} async-done(((f32[1024,512]{1,0:T(8,128)}), f32[64,512]{1,0:T(8,128)}) %reduce-scatter.9.cloned.1.call-update) | async-done | bytes 131088 | tf_op jit(solution)/shard_map/reduce_scatter | solution.py:26
  540.8 1.5 convert_element_type.16
  (4 shorter events, 0.0 us)
Async XLA Ops:
  7.2 45.5 %copy-start = (bf16[896,512]{1,0:T(8,128)(2,1)S(1)}, bf16[896,512]{1,0:T(8,128)(2,1)}, u32[]{:S(2)}) copy-start(bf16[896,512]{1,0:T(8,128)(2,1)} %param.8) | copy-start | bytes 2752516
  7.2 45.5 %all-gather.10.cloned.1.call-start = ((), (), s32[]{:S(2)}) async-start(), calls=%async_computation.7 | async-start | bytes 1114112 | tf_op jit(solution)/shard_map/all_gather | solution.py:32
  7.9 83.9 %all-gather.6.cloned.1.call-start = ((), (), s32[]{:S(2)}) async-start(), calls=%async_computation.4 | async-start | bytes 1114112 | tf_op jit(solution)/shard_map/all_gather | solution.py:11
  8.7 165.0 %reduce-scatter.15.cloned.1.call-start = ((), (), s32[]{:S(2)}) async-start(), calls=%async_computation.12 | async-start | bytes 3899392 | tf_op jit(solution)/shard_map/reduce_scatter | solution.py:34
  57.0 1.2 copy-start.1
  57.0 2.2 copy-start.2
  57.0 208.2 %reduce-scatter.13.cloned.1.call-start = ((), (), s32[]{:S(2)}) async-start(), calls=%async_computation.11 | async-start | bytes 7798784 | tf_op jit(solution)/shard_map/reduce_scatter | solution.py:15
  107.2 210.0 %all-gather.12.cloned.1.call-start = ((), (), s32[]{:S(2)}) async-start(), calls=%async_computation.8 | async-start | bytes 1949696 | tf_op jit(solution)/shard_map/all_gather | solution.py:49
  267.2 102.0 %all-gather.14.cloned.1.call-start = ((), (), s32[]{:S(2)}) async-start(), calls=%async_computation.9 | async-start | bytes 1949696 | tf_op jit(solution)/shard_map/all_gather | solution.py:50
  267.7 152.9 %all-gather.8.cloned.1.call-start = ((), (), s32[]{:S(2)}) async-start(), calls=%async_computation.5 | async-start | bytes 1949696 | tf_op jit(solution)/shard_map/all_gather | solution.py:24
  268.5 211.8 %reduce-scatter.11.cloned.1.call-start = ((), (), s32[]{:S(2)}) async-start(), calls=%async_computation.10 | async-start | bytes 2228224 | tf_op jit(solution)/shard_map/reduce_scatter | solution.py:54
  378.1 162.7 %reduce-scatter.9.cloned.1.call-start = ((), (), s32[]{:S(2)}) async-start(), calls=%async_computation.6 | async-start | bytes 2228224 | tf_op jit(solution)/shard_map/reduce_scatter | solution.py:26
  424.7 1.2 copy-start.3
Sparse Core Ops, SparseCore 0:
  9.8 42.7 all-gather.9
  54.5 37.2 all-gather.5
  95.4 78.1 reduce-scatter.14
  177.3 87.8 reduce-scatter.12
  268.3 48.7 all-gather.11
  320.3 48.7 all-gather.13
  371.8 48.7 all-gather.7
  423.4 56.8 reduce-scatter.10
  483.0 57.7 reduce-scatter.8
where the time goes:
time: 552 us; the launch traced here: 549 us
  waiting for transfers between devices  475 us (86%)
  matrix products  29.7 us (5%)
  local copies, waits for them, and re-layouts  24.6 us (4%)
  between operations  13.9 us (3%)
    reduce_scatter x1, waiting for transfers between devices, body(): lax.psum_scatter(jnp.dot(block, weights_both, preferred_element_type=jnp....  91.5 us
    reduce_scatter x1, waiting for transfers between devices, body(): lax.psum_scatter(lax.dot_general(block, down_weight, (((1,), (1,)), ((),...  66.4 us
    reduce_scatter x1, waiting for transfers between devices, body(): lax.psum_scatter(jnp.dot(block, down_weight, preferred_element_type=jnp.f...  59 us
    all_gather x1, waiting for transfers between devices, body(): lax.all_gather(up_grad, 'dp', axis=0, tiled=True)  49 us
    all_gather x1, waiting for transfers between devices, body(): lax.all_gather(gate_grad, 'dp', axis=0, tiled=True)  48.6 us
    all_gather x1, waiting for transfers between devices, body(): grad_all = lax.all_gather(out_grad, 'tensor', axis=0, tiled=True)  44 us
    all_gather x1, waiting for transfers between devices, body(): hidden_all = lax.all_gather(hidden, 'dp', axis=0, tiled=True)  42.5 us
    reduce_scatter x1, waiting for transfers between devices, body(): lax.psum_scatter(lax.dot_general(block, weights_both, (((1,), (1,)), ((),...  40 us
  transfers between devices with their start and end apart: 9, of which 9 were waited for; matrix products, arithmetic and copies ran while one was open for 10% of the time, Pallas kernels for 0%

commit v1 on v0

v1 whole, which is shorter than its diff:
```python
import math

import jax
import jax.numpy as jnp
from jax import lax
from jax.experimental import pallas as pl
from jax.experimental.pallas import tpu as pltpu
from jax.sharding import PartitionSpec as P

MIB = 1024 * 1024
BF16 = jnp.bfloat16
F32 = jnp.float32


def dot(a, b, contract):
    return lax.dot_general(a, b, ((contract[:1], contract[1:]), ((), ())), preferred_element_type=F32)


def params():
    return pltpu.CompilerParams(vmem_limit_bytes=48 * MIB)


def project(both, gate_weight, up_weight, down_weight):
    rows, width = both.shape[0], both.shape[1] // 2
    hidden = gate_weight.shape[1]
    tile = 256

    def kernel(both_ref, gate_ref, up_ref, down_ref, out_ref):
        tokens, grads = both_ref[:, :width], both_ref[:, width:]
        out_ref[:, :hidden] = dot(tokens, gate_ref[...], (1, 0)).astype(BF16)
        out_ref[:, hidden : 2 * hidden] = dot(tokens, up_ref[...], (1, 0)).astype(BF16)
        out_ref[:, 2 * hidden :] = dot(grads, down_ref[...], (1, 1)).astype(BF16)

    whole = lambda a: pl.BlockSpec(a.shape, lambda i: (0, 0))
    return pl.pallas_call(
        kernel,
        grid=(rows // tile,),
        in_specs=[
            pl.BlockSpec((tile, 2 * width), lambda i: (i, 0)),
            whole(gate_weight),
            whole(up_weight),
            whole(down_weight),
        ],
        out_specs=pl.BlockSpec((tile, 3 * hidden), lambda i: (i, 0)),
        out_shape=jax.ShapeDtypeStruct((rows, 3 * hidden), BF16),
        compiler_params=params(),
    )(both, gate_weight, up_weight, down_weight)


def activate(parts):
    count, rows, columns = parts.shape
    hidden = columns // 3
    tile = 16

    def kernel(parts_ref, out_ref):
        def total(k):
            return jnp.sum(parts_ref[:, :, k * hidden : (k + 1) * hidden].astype(F32), axis=0)

        gate, up, hidden_grad = total(0), total(1), total(2)
        s = jax.nn.sigmoid(gate)
        activated = gate * s
        out_ref[:, :hidden] = (activated * up).astype(BF16)
        out_ref[:, hidden : 2 * hidden] = (hidden_grad * up * s * (1.0 + gate * (1.0 - s))).astype(BF16)
        out_ref[:, 2 * hidden :] = (hidden_grad * activated).astype(BF16)

    return pl.pallas_call(
        kernel,
        grid=(rows // tile,),
        in_specs=[pl.BlockSpec((count, tile, columns), lambda i: (0, i, 0))],
        out_specs=pl.BlockSpec((tile, columns), lambda i: (i, 0)),
        out_shape=jax.ShapeDtypeStruct((rows, columns), BF16),
        compiler_params=params(),
    )(parts)


def back(acts, gate_weight, up_weight, down_weight):
    rows, hidden, width = acts.shape[0], gate_weight.shape[1], gate_weight.shape[0]
    tile = 256

    def kernel(acts_ref, gate_ref, up_ref, down_ref, out_ref):
        out_ref[:, :width] = dot(acts_ref[:, :hidden], down_ref[...], (1, 0))
        out_ref[:, width:] = dot(acts_ref[:, hidden : 2 * hidden], gate_ref[...], (1, 1)) + dot(
            acts_ref[:, 2 * hidden :], up_ref[...], (1, 1)
        )

    whole = lambda a: pl.BlockSpec(a.shape, lambda i: (0, 0))
    return pl.pallas_call(
        kernel,
        grid=(rows // tile,),
        in_specs=[
            pl.BlockSpec((tile, 3 * hidden), lambda i: (i, 0)),
            whole(gate_weight),
            whole(up_weight),
            whole(down_weight),
        ],
        out_specs=pl.BlockSpec((tile, 2 * width), lambda i: (i, 0)),
        out_shape=jax.ShapeDtypeStruct((rows, 2 * width), F32),
        compiler_params=params(),
    )(acts, gate_weight, up_weight, down_weight)


def weight_grads(both, acts, factor):
    rows, width, hidden = both.shape[0], both.shape[1] // 2, acts.shape[1] // 3

    def kernel(both_ref, acts_ref, gate_ref, up_ref, down_ref):
        tokens, grads = both_ref[:, :width], both_ref[:, width:]
        gate_ref[...] = dot(tokens, acts_ref[:, hidden : 2 * hidden], (0, 0)) * factor
        up_ref[...] = dot(tokens, acts_ref[:, 2 * hidden :], (0, 0)) * factor
        down_ref[...] = dot(acts_ref[:, :hidden], grads, (0, 0)) * factor

    return pl.pallas_call(
        kernel,
        out_shape=[
            jax.ShapeDtypeStruct((width, hidden), F32),
            jax.ShapeDtypeStruct((width, hidden), F32),
            jax.ShapeDtypeStruct((hidden, width), F32),
        ],
        compiler_params=params(),
    )(both, acts)


def body(tokens, gate_weight, up_weight, down_weight, out_grad):
    shard, width = tokens.shape
    tensor = lax.axis_size("tensor")
    dp = lax.axis_size("dp")
    rows = shard * tensor
    core = lax.axis_index("tensor") % 2
    both = lax.all_gather(jnp.concatenate([tokens, out_grad], 1), "tensor", axis=0, tiled=True)
    both = both.reshape(tensor // 2, 2, shard, 2 * width).transpose(1, 0, 2, 3).reshape(rows, 2 * width)
    partials = project(both, gate_weight, up_weight, down_weight)
    parts = lax.all_to_all(partials, "dp", 0, 0, tiled=True)
    acts = activate(parts.reshape(dp, rows // dp, parts.shape[1]))
    acts = lax.all_gather(acts, "dp", axis=0, tiled=True)
    sums = back(acts, gate_weight, up_weight, down_weight)
    half = rows // 2
    mine = lax.dynamic_slice_in_dim(sums, core * half, half, 0)
    other = lax.dynamic_slice_in_dim(sums, (1 - core) * half, half, 0)
    other = lax.ppermute(other, "tensor", [(i, i ^ 1) for i in range(tensor)])
    groups = [[z * 2 + c for z in range(tensor // 2)] for c in range(2)]
    result = lax.psum_scatter(mine + other, "tensor", scatter_dimension=0, tiled=True, axis_index_groups=groups).astype(BF16)
    grads = weight_grads(both, acts, 1.0 / math.sqrt(rows))
    return (result[:, :width], result[:, width:], *grads)


def solution(mesh):
    return jax.shard_map(
        body,
        mesh=mesh,
        in_specs=(
            P("tensor", "dp"),
            P("dp", "tensor"),
            P("dp", "tensor"),
            P("tensor", "dp"),
            P("tensor", "dp"),
        ),
        out_specs=(
            P("tensor", "dp"),
            P("tensor", "dp"),
            P("dp", "tensor"),
            P("dp", "tensor"),
            P("tensor", "dp"),
        ),
        check_vma=False,
    )
```

time: 552 us -> 264 us (0.48)
  waiting for transfers between devices: 475 us -> 138 us
  blocking collectives: 0 us -> 71 us
  matrix products: 29.7 us -> 0 us
  Pallas kernels: 0 us -> 21.8 us
  local copies, waits for them, and re-layouts: 24.6 us -> 8.52 us
    reduce_scatter x4 -> x1, waiting for transfers between devices: 257 us -> 30.4 us  [body(): lax.psum_scatter(mine + other, 'tensor', scatter_dimension=0, tiled=True,...]
    all_gather x5 -> x2, waiting for transfers between devices: 216 us -> 104 us  [the longest x1 58.1 us: body(): acts = lax.all_gather(acts, 'dp', axis=0, tiled=True)]
    all_to_all x0 -> x1, blocking collectives: none -> 71 us  [body(): parts = lax.all_to_all(partials, 'dp', 0, 0, tiled=True)]
    dot_general x5 -> x0, matrix products: 25.4 us -> none  [the longest x1 6.93 us: body(): jnp.dot(block, weights_both, preferred_element_type=jnp.float32)]
    pallas_call x0 -> x4, Pallas kernels: none -> 21.8 us  [the longest x1 7.24 us: weight_grads(): pl.pallas_call(kernel, out_shape=[jax.ShapeDtypeStruct((width, hidden), F...]
    unnamed x13 -> x10, local copies, waits for them, and re-layouts: 19.1 us -> 2.73 us
  transfers between devices with their start and end apart: 9 -> 4, of which waited for: 9 -> 4; matrix products, arithmetic and copies ran while one was open for 10% -> 0% of each run, Pallas kernels for 0% -> 3%
where the time goes in v1:
time: 264 us; the launch traced here: 261 us
  waiting for transfers between devices  138 us (52%)
  blocking collectives  71 us (27%)
  Pallas kernels  21.8 us (8%)
  between operations  13.8 us (5%)
  local copies, waits for them, and re-layouts  8.52 us (3%)
  other arithmetic  6.59 us (2%)
    all_to_all x1, blocking collectives, body(): parts = lax.all_to_all(partials, 'dp', 0, 0, tiled=True)  71 us
    all_gather x1, waiting for transfers between devices, body(): acts = lax.all_gather(acts, 'dp', axis=0, tiled=True)  58.1 us
    all_gather x1, waiting for transfers between devices, body(): lax.all_gather(jnp.concatenate([tokens, out_grad], 1), 'tensor', axis=0,...  45.6 us
    reduce_scatter x1, waiting for transfers between devices, body(): lax.psum_scatter(mine + other, 'tensor', scatter_dimension=0, tiled=True,...  30.4 us
    pallas_call x1, Pallas kernels, weight_grads(): pl.pallas_call(kernel, out_shape=[jax.ShapeDtypeStruct((width, hidden), F...  7.24 us
    pallas_call x1, Pallas kernels, back(): pl.pallas_call(kernel, grid=(rows // tile,), in_specs=[pl.BlockSpec((tile...  7.15 us
  transfers between devices with their start and end apart: 4, of which 4 were waited for; matrix products, arithmetic and copies ran while one was open for 0% of the time, Pallas kernels for 3%

profile of v1, /device:TPU:1, one launch (start us, length us, event | category | flops | bytes accessed | tf_op | source)
XLA Modules:
  0.0 260.7 jit_solution(13558318878119681520)
XLA Ops:
  7.2 0.0 all-gather.3.cloned.1.call-start
  7.2 1.5 pad_maximum_fusion
  8.7 0.0 all-gather.3.cloned.1.call-update
  8.8 0.0 all-gather.5.cloned.1.call-start
  8.8 45.6 %all-gather.3.cloned.1.call-done = bf16[1024,1024]{1,0:T(8,128)(2,1)} async-done(((bf16[64,1024]{1,0:T(8,128)(2,1)}), bf16[1024,1024]{1,0:T(8,128)(2,1)}) %all-gather.3.cloned.1.call-update) | async-done | bytes 2097168 | tf_op jit(solution)/shard_map/all_gather | solution.py:128
  54.4 0.0 copy-start
  54.4 0.0 copy-start.1
  54.4 0.0 copy-start.3
  54.4 2.0 copy.10
  56.4 0.0 copy-done
  56.4 0.1 copy-done.1
  56.5 0.3 copy-done.3
  56.8 5.2 %shard_map.92 = bf16[1024,2688]{1,0:T(8,128)(2,1)} custom-call(bf16[1024,1024]{1,0:T(8,128)(2,1)S(1)} %bitcast.5, bf16[512,896]{1,0:T(8,128)(2,1)S(1)} %copy-done, bf16[512,896]{1,0:T(8,128)(2,1)S(1)} %copy-done.1, bf16[896,512]{1,0:T(8,128)(2,1)S(1)} %copy-done.3), custom_call_target="tpu_custom_call" | custom-call | tf_op jit(solution)/shard_map/pallas_call | solution.py:35
  61.9 71.0 %all_to_all.9.parts_ref = bf16[16,64,2688]{2,1,0:T(8,128)(2,1)S(1)} all-to-all(bf16[16,64,2688]{2,1,0:T(8,128)(2,1)} %bitcast.7), channel_id=1, replica_groups=mesh['dp'=16,'tensor'=16] {'dp'}, dimensions={0} | all-to-all | bytes 11010048 | tf_op jit(solution)/shard_map/all_to_all | solution.py:131
  133.0 2.2 shard_map.93
  135.2 0.0 all-gather.5.cloned.1.call-update
  135.2 0.0 reduce-scatter.2.cloned.1.call-start
  135.3 58.1 %all-gather.5.cloned.1.call-done.acts_ref = bf16[1024,2688]{1,0:T(8,128)(2,1)} async-done(((bf16[64,2688]{1,0:T(8,128)(2,1)}), bf16[1024,2688]{1,0:T(8,128)(2,1)}) %all-gather.5.cloned.1.call-update) | async-done | bytes 5505040 | tf_op jit(solution)/shard_map/all_gather | solution.py:133
  193.3 0.0 copy-start.2
  193.3 1.2 copy-done.2
  194.5 0.0 copy-start.4
  194.5 1.2 copy-done.4
  195.7 7.2 %shard_map.94 = f32[1024,1024]{1,0:T(8,128)} custom-call(bf16[1024,2688]{1,0:T(8,128)(2,1)} %all-gather.5.cloned.1.call-done.acts_ref, bf16[512,896]{1,0:T(8,128)(2,1)S(1)} %copy-done, bf16[512,896]{1,0:T(8,128)(2,1)S(1)} %copy-done.2, bf16[896,512]{1,0:T(8,128)(2,1)S(1)} %copy-done.4), custom_call_target="tpu_custom_call" | custom-call | tf_op jit(solution)/shard_map/pallas_call | solution.py:87
  202.8 3.2 %constant_dynamic-slice_fusion = f32[512,1024]{1,0:T(8,128)} fusion(f32[1024,1024]{1,0:T(8,128)} %shard_map.94, s32[]{:T(128)S(6)} %select_n.15), kind=kLoop, calls=%fused_computation.2 | loop fusion | bytes 4194308 | tf_op jit(solution)/shard_map/dynamic_slice | solution.py:137
  206.0 0.7 collective-permute-start
  206.7 4.1 %collective-permute-done = f32[512,1024]{1,0:T(8,128)} collective-permute-done((f32[512,1024]{1,0:T(8,128)}, f32[512,1024]{1,0:T(8,128)}, u32[]{:S(2)}, u32[]{:S(2)}) %collective-permute-start) | collective-permute-done | bytes 2097184 | tf_op jit(solution)/shard_map/ppermute | solution.py:138
  210.8 4.1 %dynamic-slice_add_fusion = f32[512,1024]{1,0:T(8,128)} fusion(f32[512,1024]{1,0:T(8,128)} %collective-permute-done, f32[1024,1024]{1,0:T(8,128)} %shard_map.94, s32[]{:T(128)S(6)} %select_n.14), kind=kLoop, calls=%fused_computation | loop fusion | flops 524288 | bytes 6291460 | tf_op jit(solution)/shard_map/add | solution.py:140
  214.9 0.0 reduce-scatter.2.cloned.1.call-update
  214.9 7.2 %shard_map.95 = (f32[512,896]{1,0:T(8,128)}, f32[512,896]{1,0:T(8,128)}, f32[896,512]{1,0:T(8,128)}) custom-call(bf16[1024,1024]{1,0:T(8,128)(2,1)S(1)} %bitcast.6, bf16[1024,2688]{1,0:T(8,128)(2,1)} %all-gather.5.cloned.1.call-done.acts_ref), custom_call_target="tpu_custom_call" | custom-call | tf_op jit(solution)/shard_map/pallas_call | solution.py:111
  222.1 30.4 %reduce-scatter.2.cloned.1.call-done = f32[64,1024]{1,0:T(8,128)} async-done(((f32[512,1024]{1,0:T(8,128)}), f32[64,1024]{1,0:T(8,128)}) %reduce-scatter.2.cloned.1.call-update) | async-done | bytes 262160 | tf_op jit(solution)/shard_map/reduce_scatter | solution.py:140
  252.6 1.0 convert_element_type.3
  253.5 0.7 fusion
Async XLA Ops:
  7.2 47.2 %all-gather.3.cloned.1.call-start = ((), (), s32[]{:S(2)}) async-start(), calls=%async_computation.2 | async-start | bytes 2228224 | tf_op jit(solution)/shard_map/all_gather | solution.py:128
  8.8 184.5 %all-gather.5.cloned.1.call-start = ((), (), s32[]{:S(2)}) async-start(), calls=%async_computation.3 | async-start | bytes 5849088 | tf_op jit(solution)/shard_map/all_gather | solution.py:133
  54.4 2.0 copy-start
  54.4 2.1 copy-start.1
  54.4 2.4 copy-start.3
  135.2 117.4 %reduce-scatter.2.cloned.1.call-start = ((), (), s32[]{:S(2)}) async-start(), calls=%async_computation.4 | async-start | bytes 2359296 | tf_op jit(solution)/shard_map/reduce_scatter | solution.py:140
  193.3 1.2 copy-start.2
  194.5 1.2 copy-start.4
  206.0 4.8 %collective-permute-start = (f32[512,1024]{1,0:T(8,128)}, f32[512,1024]{1,0:T(8,128)}, u32[]{:S(2)}, u32[]{:S(2)}) collective-permute-start(f32[512,1024]{1,0:T(8,128)} %constant_dynamic-slice_fusion), channel_id=1, source_target_pairs={{0,1},{1,0},{2,3},{3,2},{4,5},{5,4},{6,7},{7,6},{8,9},{9,8},{10,11... | collective-permute-start | bytes 6291464 | tf_op jit(solution)/shard_map/ppermute | solution.py:138
Sparse Core Ops, SparseCore 0:
  10.4 43.9 all-gather.2
  135.3 57.9 all-gather.4
  215.0 37.4 reduce-scatter.1
